TPU v7x, 512 devices: a whole 4x8x8 slice. The times are simulated.
512 devices in a mesh: ctx: 64 (over x, z, core), tp: 8 (over y).
Axes of the slice: x: 4, y: 8, z: 8, core: 2. Of those that a mesh axis runs over, the one named last changes fastest.
Arguments:
- features: bfloat16 [128, 196, 1152], P('ctx', None, 'tp'), may hold values from -6 to 6
- group_kernel: bfloat16 [9, 1152, 48], P(None, 'tp'), may hold values from -0.3125 to 0.3125
- squeeze_in: bfloat16 [1152, 288], P('tp'), may hold values from -0.75 to 0.75
- squeeze_out: bfloat16 [288, 1152], P(None, 'tp'), may hold values from -0.75 to 0.75
- sampler_kernel: bfloat16 [1152, 8, 1152], P('ctx', None, 'tp'), may hold values from -0.0625 to 0.0625
- readout_kernel: bfloat16 [1152, 8192], P('ctx', 'tp'), may hold values from -0.1875 to 0.1875
- frame_clip: int32 [128], replicated, may hold values from 0 to 15, as said below
- clip_keep: int32 [16], replicated, may hold values from 1 to 512, as said below
- token_cotangent: bfloat16 [4096, 8192], P('ctx', 'tp'), may hold values from -6 to 6
Outputs:
- llm_tokens: bfloat16 [4096, 8192], P('ctx', 'tp')
- grad_features: bfloat16 [128, 196, 1152], P('ctx', None, 'tp')
Inputs may be any that keep to these rules, and one draw needn't show every extreme that they name: `frame_clip`: clip ids start at 0 and never fall along the frames; every clip covers an even number of frames from 2 to 16 and starts at an even frame; some clip covers 16. `clip_keep`: each clip keeps at least one and at most 8 * 8 times half its frames of its tokens; the clip of 16 frames keeps all of its tokens, and some clip keeps a single token.
All inputs are finite; a program needn't handle non-finite values.
Results may differ from a plain program's by a relative error of at most 0.009.
Values may be sent and summed in bfloat16 or wider, within the bound.
A program may use at most 64 MiB of HBM per device.

v0:
```python
import jax
import jax.numpy as jnp
from jax import lax
from jax.sharding import PartitionSpec as P

SIDE = 14
OUT_SIDE = 8


def shifted(value, axis, by):
    count = lax.axis_size(axis)
    pairs = [(i, i + by) for i in range(count) if 0 <= i + by < count]
    return lax.ppermute(value, axis, pairs)


def silu_slope(values):
    sigma = jax.nn.sigmoid(values)
    return sigma * (1.0 + values * (1.0 - sigma))


def grouped_forward(frames_grid, group_kernel):
    count, side, _, chans = frames_grid.shape
    width = group_kernel.shape[2]
    groups = chans // width
    padded = jnp.pad(frames_grid, ((0, 0), (1, 1), (1, 1), (0, 0)))
    kernel = group_kernel.reshape(9, groups, width, width)
    total = jnp.zeros((count, side, side, groups, width), jnp.float32)
    for kernel_tap in range(9):
        row_shift, col_shift = divmod(kernel_tap, 3)
        window = padded[:, row_shift : row_shift + side, col_shift : col_shift + side]
        window = window.reshape(count, side, side, groups, width)
        total = total + jnp.einsum(
            "fyxgi,gio->fyxgo", window, kernel[kernel_tap], preferred_element_type=jnp.float32
        )
    return total.reshape(count, side, side, chans)


def grouped_backward(grad_grid, group_kernel):
    count, side, _, chans = grad_grid.shape
    width = group_kernel.shape[2]
    groups = chans // width
    kernel = group_kernel.reshape(9, groups, width, width)
    source = grad_grid.reshape(count, side, side, groups, width)
    total = jnp.zeros((count, side + 2, side + 2, chans), jnp.float32)
    for kernel_tap in range(9):
        row_shift, col_shift = divmod(kernel_tap, 3)
        spread = jnp.einsum(
            "fyxgo,gio->fyxgi", source, kernel[kernel_tap], preferred_element_type=jnp.float32
        )
        spread = spread.reshape(count, side, side, chans)
        total = total + jnp.pad(
            spread, ((0, 0), (row_shift, 2 - row_shift), (col_shift, 2 - col_shift), (0, 0))
        )
    return total[:, 1 : side + 1, 1 : side + 1]


def make_patches(prev_odd, even):
    stacked = jnp.stack([prev_odd, even], axis=1)
    stacked = jnp.pad(stacked, ((0, 0), (0, 0), (1, 1), (1, 1), (0, 0)))
    pairs, _, padded_side, _, chans = stacked.shape
    half = padded_side // 2
    shaped = stacked.reshape(pairs, 2, half, 2, half, 2, chans).transpose(0, 2, 4, 1, 3, 5, 6)
    return shaped.reshape(pairs * half * half, 8 * chans)


def unpatch(grad_rows, pairs, side, chans):
    half = side // 2 + 1
    shaped = grad_rows.reshape(pairs, half, half, 2, 2, 2, chans).transpose(0, 3, 1, 4, 2, 5, 6)
    shaped = shaped.reshape(pairs, 2, 2 * half, 2 * half, chans)
    return shaped[:, :, 1 : side + 1, 1 : side + 1]


def contract_last(left, right):
    return lax.dot_general(
        left, right, (((1,), (1,)), ((), ())), preferred_element_type=jnp.float32
    )


def per_device(
    features,
    group_kernel,
    squeeze_in,
    squeeze_out,
    sampler_kernel,
    readout_kernel,
    frame_clip,
    clip_keep,
    token_cotangent,
):
    highest = lax.Precision.HIGHEST
    shard_index = lax.axis_index("ctx")
    frames_dev, cells, chans = features.shape
    pairs_dev = frames_dev // 2
    grid = features.reshape(frames_dev, SIDE, SIDE, chans)
    conv_out = grouped_forward(grid, group_kernel)
    active = jax.nn.silu(conv_out)
    pooled = jnp.mean(active, axis=(1, 2))
    squeezed = lax.psum(jnp.dot(pooled, squeeze_in.astype(jnp.float32), precision=highest), "tp")
    relaxed = jax.nn.silu(squeezed)
    excite = jax.nn.sigmoid(jnp.dot(relaxed, squeeze_out.astype(jnp.float32), precision=highest))
    hidden = (grid.astype(jnp.float32) + active * excite[:, None, None, :]).astype(jnp.bfloat16)
    full_sampler, full_readout = (
        lax.all_gather(sampler_kernel, "ctx", axis=0, tiled=True),
        lax.all_gather(readout_kernel, "ctx", axis=0, tiled=True),
    )
    sampler_rows = full_sampler.reshape(full_sampler.shape[0], 8 * chans)
    halo_frame = shifted(hidden[-1], "ctx", 1)
    local_clip = lax.dynamic_slice_in_dim(frame_clip, shard_index * frames_dev, frames_dev)
    edge_clip = lax.dynamic_slice_in_dim(
        frame_clip, jnp.maximum(shard_index * frames_dev - 1, 0), 1
    )
    first_keep = jnp.logical_and(shard_index > 0, edge_clip[0] == local_clip[0])
    later_keep = local_clip[1:-1:2] == local_clip[2::2]
    pair_mask = jnp.concatenate([first_keep[None], later_keep]).astype(jnp.float32)
    even = hidden[0::2]
    odd = hidden[1::2]
    prev_odd = jnp.concatenate([halo_frame[None], odd[:-1]], axis=0)
    prev_odd = prev_odd * pair_mask.astype(jnp.bfloat16)[:, None, None, None]
    patches = make_patches(prev_odd, even)
    per_frame = OUT_SIDE * OUT_SIDE
    pair_clip = frame_clip[0::2]
    clip_ids = jnp.arange(clip_keep.shape[0], dtype=jnp.int32)
    start_pair = jnp.sum((pair_clip[None, :] < clip_ids[:, None]).astype(jnp.int32), axis=1)
    own_clip = local_clip[0::2]
    one_hot = (own_clip[:, None] == clip_ids[None, :]).astype(jnp.int32)
    own_start = jnp.sum(one_hot * start_pair[None, :], axis=1)
    own_keep = jnp.sum(one_hot * clip_keep[None, :], axis=1)
    pair_index = shard_index * pairs_dev + jnp.arange(pairs_dev, dtype=jnp.int32)
    position = (pair_index - own_start)[:, None] * per_frame + jnp.arange(
        per_frame, dtype=jnp.int32
    )[None, :]
    live = (position < own_keep[:, None]).reshape(-1).astype(jnp.bfloat16)
    pre = lax.psum(contract_last(patches, sampler_rows), "tp")
    act = jax.nn.silu(pre).astype(jnp.bfloat16)
    tokens = (
        jnp.dot(act, full_readout, preferred_element_type=jnp.float32).astype(jnp.bfloat16)
        * live[:, None]
    )
    llm_tokens = lax.all_to_all(tokens, "ctx", split_axis=0, concat_axis=0, tiled=True)
    back = (
        lax.all_to_all(token_cotangent, "ctx", split_axis=0, concat_axis=0, tiled=True)
        * live[:, None]
    )
    grad_act = lax.psum(contract_last(back, full_readout), "tp")
    grad_pre = (grad_act * silu_slope(pre)).astype(jnp.bfloat16)
    grad_patches = jnp.dot(grad_pre, sampler_rows, preferred_element_type=jnp.float32)
    grad_taps = unpatch(grad_patches, pairs_dev, SIDE, chans)
    leading = grad_taps[:, 0] * pair_mask[:, None, None, None]
    incoming = shifted(leading[0].astype(jnp.bfloat16), "ctx", -1).astype(jnp.float32)
    grad_even = grad_taps[:, 1]
    grad_odd = jnp.concatenate([leading[1:], incoming[None]], axis=0)
    grad_hidden = jnp.stack([grad_even, grad_odd], axis=1).reshape(frames_dev, SIDE, SIDE, chans)
    grad_excite = jnp.sum(grad_hidden * active, axis=(1, 2))
    grad_inner = grad_excite * excite * (1.0 - excite)
    grad_relaxed = lax.psum(
        jnp.dot(grad_inner, squeeze_out.astype(jnp.float32).T, precision=highest), "tp"
    )
    grad_squeezed = grad_relaxed * silu_slope(squeezed)
    grad_pooled = jnp.dot(grad_squeezed, squeeze_in.astype(jnp.float32).T, precision=highest)
    grad_active = grad_hidden * excite[:, None, None, :] + grad_pooled[:, None, None, :] / cells
    grad_conv = (grad_active * silu_slope(conv_out)).astype(jnp.bfloat16)
    grad_grid = grad_hidden + grouped_backward(grad_conv, group_kernel)
    grad_features = grad_grid.astype(jnp.bfloat16).reshape(frames_dev, cells, chans)
    return (llm_tokens, grad_features)


def solution(mesh):
    placed = (
        P("ctx", None, "tp"),
        P(None, "tp", None),
        P("tp", None),
        P(None, "tp"),
        P("ctx", None, "tp"),
        P("ctx", "tp"),
        P(),
        P(),
        P("ctx", "tp"),
    )
    return jax.shard_map(
        per_device,
        mesh=mesh,
        in_specs=placed,
        out_specs=(P("ctx", "tp"), P("ctx", None, "tp")),
        check_vma=False,
    )
```

profile of v0, /device:TPU:6, one launch (start us, length us, event | category | flops | bytes accessed | tf_op | source)
XLA Modules:
  0.0 348.0 jit_solution(8308310035529797624)
XLA Ops:
  12.4 2.3 pad_slice_fusion
  19.0 2.0 reshape.192
  21.2 2.0 reshape.193
  27.1 17.6 %psum.28 = f32[2,288]{1,0:T(2,128)S(1)} all-reduce(f32[2,288]{1,0:T(2,128)S(1)} %fusion.54), channel_id=1, replica_groups=mesh['ctx'=64,'tp'=8] {'tp'}, use_global_device_ids=true, to_apply=%region_1.2 | all-reduce | flops 576 | bytes 4608 | tf_op jit(solution)/shard_map/psum | solution.py:98
  47.2 1.9 collective-permute-start
  51.1 15.2 %all-to-all-start.1 = ((bf16[64,2,512]{2,1,0:T(2,128)(2,1)}), bf16[64,2,512]{2,1,0:T(2,128)(2,1)S(1)}, u32[]{:S(2)}, u32[]{:S(2)}) async-start(bf16[64,2,512]{2,1,0:T(2,128)(2,1)} %reshape.225), calls=%async_computation.1 | async-start | bytes 262144 | tf_op jit(solution)/shard_map/all_to_all | solution.py:141
  72.5 2.6 all-to-all-done.1
  75.3 24.2 %all-gather.6.cloned.1.call-done = bf16[64,18,1024]{2,1,0:T(8,128)(2,1)} async-done(((bf16[1,18,1024]{2,1,0:T(8,128)(2,1)}), bf16[64,18,1024]{2,1,0:T(8,128)(2,1)}) %all-gather.6.cloned.1.call-update) | async-done | bytes 2359312 | tf_op jit(solution)/shard_map/all_gather | solution.py:104
  99.5 2.9 reshape.212
  102.4 1.6 fusion.29
  104.0 81.3 %all-gather.4.cloned.1.call-done = bf16[1152,8,144]{2,1,0:T(8,128)(2,1)} async-done(((bf16[18,8,144]{2,1,0:T(8,128)(2,1)}), bf16[1152,8,144]{2,1,0:T(8,128)(2,1)}) %all-gather.4.cloned.1.call-update) | async-done | bytes 2654224 | tf_op jit(solution)/shard_map/all_gather | solution.py:103
  185.3 5.5 %copy.254 = bf16[1152,8,144]{0,2,1:T(8,128)(2,1)S(1)} copy(bf16[1152,8,144]{2,1,0:T(8,128)(2,1)} %all-gather.4.cloned.1.call-done) | data formatting | bytes 5308416 | tf_op jit(solution)/shard_map/all_gather | solution.py:103
  190.8 2.2 fusion.55
  193.1 77.1 %all-reduce.14.cloned.1.call-done = (f32[64,1152]{1,0:T(8,128)}, f32[64,1152]{1,0:T(8,128)}) async-done(((f32[64,1152]{1,0:T(8,128)}, f32[64,1152]{1,0:T(8,128)}), (f32[64,1152]{1,0:T(8,128)}, f32[64,1152]{1,0:T(8,128)})) %all-reduce.14.cloned.1.call-update) | async-done | bytes 589840 | tf_op jit(solution)/shard_map/psum | solution.py:144
  270.3 2.3 convolution_bitcast_fusion.14
  273.8 2.1 collective-permute-start.1
  278.1 11.2 %all-to-all-start = ((bf16[64,2,512]{2,1,0:T(2,128)(2,1)}), bf16[64,2,512]{2,1,0:T(2,128)(2,1)S(1)}, u32[]{:S(2)}, u32[]{:S(2)}) async-start(bf16[64,2,512]{2,1,0:T(2,128)(2,1)} %reshape.227), calls=%async_computation | async-start | bytes 262144 | tf_op jit(solution)/shard_map/all_to_all | solution.py:139
  290.1 16.7 %psum.31 = f32[2,288]{1,0:T(2,128)S(1)} all-reduce(f32[2,288]{1,0:T(2,128)S(1)} %fusion.39), channel_id=1, replica_groups=mesh['ctx'=64,'tp'=8] {'tp'}, use_global_device_ids=true, to_apply=%region_8.9 | all-reduce | flops 576 | bytes 4608 | tf_op jit(solution)/shard_map/psum | solution.py:155
  316.2 1.5 copy.264
  319.0 1.5 copy.265
  321.9 1.5 copy.266
  324.8 1.5 copy.267
  335.9 1.5 pad_add_fusion
  337.4 2.4 fusion.15
  (180 shorter events, 51.3 us)
Async XLA Ops:
  7.2 38.1 %copy-start = (bf16[288,144]{0,1:T(8,128)(2,1)S(1)}, bf16[288,144]{0,1:T(8,128)(2,1)}, u32[]{:S(2)}) copy-start(bf16[288,144]{0,1:T(8,128)(2,1)} %param.12) | copy-start | bytes 248836
  7.2 92.3 %all-gather.6.cloned.1.call-start = ((), (), s32[]{:S(2)}) async-start(), calls=%async_computation.3 | async-start | bytes 3194880 | tf_op jit(solution)/shard_map/all_gather | solution.py:104
  7.9 177.4 %all-gather.4.cloned.1.call-start = ((), (), s32[]{:S(2)}) async-start(), calls=%async_computation.2 | async-start | bytes 4792320 | tf_op jit(solution)/shard_map/all_gather | solution.py:103
  15.1 8.3 %copy-start.9 = (bf16[1,144,48]{2,1,0:T(8,128)(2,1)}, bf16[1,144,48]{2,1,0:T(8,128)(2,1)S(1)}, u32[]{:S(2)}) copy-start(bf16[1,144,48]{2,1,0:T(8,128)(2,1)S(1)} %copy.233) | copy-start | bytes 41476
  15.5 8.2 %copy-start.11 = (bf16[1,144,48]{2,1,0:T(8,128)(2,1)}, bf16[1,144,48]{2,1,0:T(8,128)(2,1)S(1)}, u32[]{:S(2)}) copy-start(bf16[1,144,48]{2,1,0:T(8,128)(2,1)S(1)} %copy.235) | copy-start | bytes 41476
  15.8 8.0 %copy-start.13 = (bf16[1,144,48]{2,1,0:T(8,128)(2,1)}, bf16[1,144,48]{2,1,0:T(8,128)(2,1)S(1)}, u32[]{:S(2)}) copy-start(bf16[1,144,48]{2,1,0:T(8,128)(2,1)S(1)} %copy.237) | copy-start | bytes 41476
  16.2 7.9 %copy-start.15 = (bf16[1,144,48]{2,1,0:T(8,128)(2,1)}, bf16[1,144,48]{2,1,0:T(8,128)(2,1)S(1)}, u32[]{:S(2)}) copy-start(bf16[1,144,48]{2,1,0:T(8,128)(2,1)S(1)} %copy.239) | copy-start | bytes 41476
  16.6 7.8 %copy-start.17 = (bf16[1,144,48]{2,1,0:T(8,128)(2,1)}, bf16[1,144,48]{2,1,0:T(8,128)(2,1)S(1)}, u32[]{:S(2)}) copy-start(bf16[1,144,48]{2,1,0:T(8,128)(2,1)S(1)} %copy.242) | copy-start | bytes 41476
  16.9 7.7 %copy-start.19 = (bf16[1,144,48]{2,1,0:T(8,128)(2,1)}, bf16[1,144,48]{2,1,0:T(8,128)(2,1)S(1)}, u32[]{:S(2)}) copy-start(bf16[1,144,48]{2,1,0:T(8,128)(2,1)S(1)} %copy.244) | copy-start | bytes 41476
  19.0 5.9 %copy-start.21 = (bf16[1,144,48]{2,1,0:T(8,128)(2,1)}, bf16[1,144,48]{2,1,0:T(8,128)(2,1)S(1)}, u32[]{:S(2)}) copy-start(bf16[1,144,48]{2,1,0:T(8,128)(2,1)S(1)} %copy.246) | copy-start | bytes 41476
  25.8 23.9 %copy-start.25 = (bf16[64,1024]{1,0:T(8,128)(2,1)S(1)}, bf16[64,1024]{1,0:T(8,128)(2,1)}, u32[]{:S(2)}) copy-start(bf16[64,1024]{1,0:T(8,128)(2,1)} %param.17) | copy-start | bytes 393220
  26.3 40.2 %copy-start.33 = (s32[128]{0:T(128)S(1)}, s32[128]{0:T(128)}, u32[]{:S(2)}) copy-start(s32[128]{0:T(128)} %param.15) | copy-start | bytes 1540
  26.3 43.2 %copy-start.34 = (s32[16]{0:T(128)S(1)}, s32[16]{0:T(128)}, u32[]{:S(2)}) copy-start(s32[16]{0:T(128)} %param.16) | copy-start | bytes 196
  47.2 23.6 %collective-permute-start = (bf16[14,14,144]{2,1,0:T(8,128)(2,1)S(1)}, bf16[14,14,144]{2,1,0:T(8,128)(2,1)S(1)}, u32[]{:S(2)}, u32[]{:S(2)}) collective-permute-start(bf16[14,14,144]{2,1,0:T(8,128)(2,1)S(1)} %bitcast.239), channel_id=1, source_target_pairs={{0,8},{8,16},{16,24},{24,32},{32,40},{40,48},{48,56},{56,64},{64,7... | collective-permute-start | bytes 169352 | tf_op jit(solution)/shard_map/ppermute | solution.py:13
  51.1 24.1 %all-to-all-start.1 = ((bf16[64,2,512]{2,1,0:T(2,128)(2,1)}), bf16[64,2,512]{2,1,0:T(2,128)(2,1)S(1)}, u32[]{:S(2)}, u32[]{:S(2)}) async-start(bf16[64,2,512]{2,1,0:T(2,128)(2,1)} %reshape.225), calls=%async_computation.1 | async-start | bytes 262144 | tf_op jit(solution)/shard_map/all_to_all | solution.py:141
  66.3 204.0 %all-reduce.14.cloned.1.call-start = ((), (), s32[]{:S(2)}) async-start(), calls=%async_computation.4 | async-start | bytes 1179648 | tf_op jit(solution)/shard_map/psum | solution.py:144
  70.8 31.6 %copy-start.30 = (bf16[64]{0:T(256)(128)(2,1)}, bf16[64]{0:T(256)(128)(2,1)S(1)}, u32[]{:S(2)}) copy-start(bf16[64]{0:T(256)(128)(2,1)S(1)} %compare_convert_fusion) | copy-start | bytes 388
  273.8 15.7 %copy-start.3 = (f32[2,14,14,144]{3,0,2,1:T(2,128)S(1)}, f32[2,14,14,144]{3,0,2,1:T(2,128)}, u32[]{:S(2)}) copy-start(f32[2,14,14,144]{3,0,2,1:T(2,128)} %get-tuple-element.17) | copy-start | bytes 677380
  273.8 33.1 %copy-start.27 = (bf16[144,288]{1,0:T(8,128)(2,1)S(1)}, bf16[144,288]{1,0:T(8,128)(2,1)}, u32[]{:S(2)}) copy-start(bf16[144,288]{1,0:T(8,128)(2,1)} %param.11) | copy-start | bytes 248836
  273.8 33.1 %copy-start.29 = (f32[2,288]{1,0:T(2,128)S(1)}, f32[2,288]{1,0:T(2,128)}, u32[]{:S(2)}) copy-start(f32[2,288]{1,0:T(2,128)} %copy-done.28) | copy-start | bytes 6916
  273.8 15.5 %collective-permute-start.1 = (bf16[14,14,144]{2,1,0:T(8,128)(2,1)S(1)}, bf16[14,14,144]{2,1,0:T(8,128)(2,1)S(1)}, u32[]{:S(2)}, u32[]{:S(2)}) collective-permute-start(bf16[14,14,144]{2,1,0:T(8,128)(2,1)S(1)} %fusion.31), channel_id=1, source_target_pairs={{8,0},{16,8},{24,16},{32,24},{40,32},{48,40},{56,48},{64,56},{72,6... | collective-permute-start | bytes 169352 | tf_op jit(solution)/shard_map/ppermute | solution.py:13
  278.1 62.5 %all-to-all-start = ((bf16[64,2,512]{2,1,0:T(2,128)(2,1)}), bf16[64,2,512]{2,1,0:T(2,128)(2,1)S(1)}, u32[]{:S(2)}, u32[]{:S(2)}) async-start(bf16[64,2,512]{2,1,0:T(2,128)(2,1)} %reshape.227), calls=%async_computation | async-start | bytes 262144 | tf_op jit(solution)/shard_map/all_to_all | solution.py:139
  289.3 18.8 %copy-start.10 = (bf16[1,144,48]{2,1,0:T(8,128)(2,1)S(1)}, bf16[1,144,48]{2,1,0:T(8,128)(2,1)}, u32[]{:S(2)}) copy-start(bf16[1,144,48]{2,1,0:T(8,128)(2,1)} %copy-done.9) | copy-start | bytes 41476
  290.1 19.1 %copy-start.12 = (bf16[1,144,48]{2,1,0:T(8,128)(2,1)S(1)}, bf16[1,144,48]{2,1,0:T(8,128)(2,1)}, u32[]{:S(2)}) copy-start(bf16[1,144,48]{2,1,0:T(8,128)(2,1)} %copy-done.11) | copy-start | bytes 41476
  (18 other events, 62.1 us)
Sparse Core Ops, SparseCore 0:
  11.3 88.0 all-gather.5
  102.8 82.4 all-gather.3
  193.2 77.0 all-reduce.13
where the time goes:
time: 349 us; the launch traced here: 348 us
  waiting for transfers between devices  187 us (54%)
  local copies, waits for them, and re-layouts  54.8 us (16%)
  blocking collectives  34.3 us (10%)
  starting transfers between devices  30.7 us (9%)
  matrix products  16 us (5%)
  between operations  15.9 us (5%)
  other arithmetic  9.59 us (3%)
    all_gather x1, waiting for transfers between devices, per_device(): lax.all_gather(sampler_kernel, 'ctx', axis=0, tiled=True)  81.3 us
    psum x1, waiting for transfers between devices, per_device(): grad_act = lax.psum(contract_last(back, full_readout), 'tp')  77.1 us
    all_gather x1, waiting for transfers between devices, per_device(): lax.all_gather(readout_kernel, 'ctx', axis=0, tiled=True)  24.2 us
    psum x1, blocking collectives, per_device(): lax.psum(jnp.dot(pooled, squeeze_in.astype(jnp.float32), precision=highes...  17.6 us
    psum x1, blocking collectives, per_device(): lax.psum(jnp.dot(grad_inner, squeeze_out.astype(jnp.float32).T, precision...  16.7 us
    all_to_all x1, starting transfers between devices, per_device(): lax.all_to_all(token_cotangent, 'ctx', split_axis=0, concat_axis=0, tiled...  15.2 us
    reshape x9, local copies, waits for them, and re-layouts, grouped_backward(): spread = spread.reshape(count, side, side, chans)  12.2 us
    all_to_all x1, starting transfers between devices, per_device(): lax.all_to_all(tokens, 'ctx', split_axis=0, concat_axis=0, tiled=True)  11.2 us
  transfers between devices with their start and end apart: 7, of which 4 were waited for; matrix products, arithmetic and copies ran while one was open for 19% of the time, Pallas kernels for 0%

commit v1 on v0

--- a/solution.py
+++ b/solution.py
@@ -5,6 +5,13 @@
 
 SIDE = 14
 OUT_SIDE = 8
+
+
+def gather_over(x, axis, dim):
+    size = lax.axis_size(axis)
+    blocks = jnp.stack([x for _ in range(size)])
+    blocks = lax.all_to_all(blocks, axis, split_axis=0, concat_axis=0)
+    return jnp.concatenate(blocks, axis=dim)
 
 
 def shifted(value, axis, by):
@@ -101,7 +108,7 @@
     hidden = (grid.astype(jnp.float32) + active * excite[:, None, None, :]).astype(jnp.bfloat16)
     full_sampler, full_readout = (
         lax.all_gather(sampler_kernel, "ctx", axis=0, tiled=True),
-        lax.all_gather(readout_kernel, "ctx", axis=0, tiled=True),
+        gather_over(readout_kernel, "ctx", 0),
     )
     sampler_rows = full_sampler.reshape(full_sampler.shape[0], 8 * chans)
     halo_frame = shifted(hidden[-1], "ctx", 1)

time: 349 us -> 303 us (0.87)
  waiting for transfers between devices: 187 us -> 96.3 us
  local copies, waits for them, and re-layouts: 54.8 us -> 83.6 us
  starting transfers between devices: 30.7 us -> 35.8 us
  matrix products: 16 us -> 20.7 us
  other arithmetic: 9.59 us -> 13.9 us
    all_gather x1, waiting for transfers between devices: 81.3 us -> 0.01 us  [per_device(): lax.all_gather(sampler_kernel, 'ctx', axis=0, tiled=True)]
    all_gather x1 -> x0, waiting for transfers between devices: 24.2 us -> none  [per_device(): lax.all_gather(readout_kernel, 'ctx', axis=0, tiled=True)]
    ppermute x2, waiting for transfers between devices: 0.01 us -> 13 us  [shifted(): return lax.ppermute(value, axis, pairs)]
    reshape x9, local copies, waits for them, and re-layouts: 6.7 us -> 17.6 us  [grouped_forward(): window = window.reshape(count, side, side, groups, width)]
    slice x10, local copies, waits for them, and re-layouts: 3.24 us -> 11.9 us  [grouped_forward(): kernel[kernel_tap]]
    all_to_all x0 -> x1, starting transfers between devices: none -> 6.37 us  [gather_over(): blocks = lax.all_to_all(blocks, axis, split_axis=0, concat_axis=0)]
    unnamed x82 -> x93, local copies, waits for them, and re-layouts: 9.5 us -> 9.39 us
  transfers between devices with their start and end apart: 7 -> 7, of which waited for: 4 -> 3; matrix products, arithmetic and copies ran while one was open for 19% -> 35% of each run, Pallas kernels for 0% -> 0%
where the time goes in v1:
time: 303 us; the launch traced here: 301 us
  waiting for transfers between devices  96.3 us (32%)
  local copies, waits for them, and re-layouts  83.6 us (28%)
  starting transfers between devices  35.8 us (12%)
  blocking collectives  34.3 us (11%)
  matrix products  20.7 us (7%)
  between operations  16.2 us (5%)
  other arithmetic  13.9 us (5%)
    psum x1, waiting for transfers between devices, per_device(): grad_act = lax.psum(contract_last(back, full_readout), 'tp')  78.2 us
    reshape x9, local copies, waits for them, and re-layouts, grouped_forward(): window = window.reshape(count, side, side, groups, width)  17.6 us
    psum x1, blocking collectives, per_device(): lax.psum(jnp.dot(pooled, squeeze_in.astype(jnp.float32), precision=highes...  17.5 us
    psum x1, blocking collectives, per_device(): lax.psum(jnp.dot(grad_inner, squeeze_out.astype(jnp.float32).T, precision...  16.8 us
    all_to_all x1, starting transfers between devices, per_device(): lax.all_to_all(token_cotangent, 'ctx', split_axis=0, concat_axis=0, tiled...  14 us
    ppermute x2, waiting for transfers between devices, shifted(): return lax.ppermute(value, axis, pairs)  13 us
    reshape x9, local copies, waits for them, and re-layouts, grouped_backward(): spread = spread.reshape(count, side, side, chans)  12.2 us
    slice x10, local copies, waits for them, and re-layouts, grouped_forward(): kernel[kernel_tap]  11.9 us
  transfers between devices with their start and end apart: 7, of which 3 were waited for; matrix products, arithmetic and copies ran while one was open for 35% of the time, Pallas kernels for 0%

profile of v1, /device:TPU:6, one launch (start us, length us, event | category | flops | bytes accessed | tf_op | source)
XLA Modules:
  0.0 300.8 jit_solution(7824005747777606082)
XLA Ops:
  10.7 14.0 %all-to-all-start.2 = ((bf16[64,2,512]{2,1,0:T(2,128)(2,1)}), bf16[64,2,512]{2,1,0:T(2,128)(2,1)S(1)}, u32[]{:S(2)}, u32[]{:S(2)}) async-start(bf16[64,2,512]{2,1,0:T(2,128)(2,1)} %reshape.236), calls=%async_computation.2 | async-start | bytes 262144 | tf_op jit(solution)/shard_map/all_to_all | solution.py:148
  29.2 4.4 %all-to-all-done.2 = bf16[64,2,512]{2,1,0:T(2,128)(2,1)S(1)} async-done(((bf16[64,2,512]{2,1,0:T(2,128)(2,1)}), bf16[64,2,512]{2,1,0:T(2,128)(2,1)S(1)}, u32[]{:S(2)}, u32[]{:S(2)}) %all-to-all-start.2) | async-done | bytes 131104 | tf_op jit(solution)/shard_map/all_to_all | solution.py:148
  33.6 2.9 stack.19
  36.5 6.4 %all-to-all-start = ((bf16[64,18,1024]{2,1,0:T(8,128)(2,1)}), bf16[64,18,1024]{2,1,0:T(8,128)(2,1)S(1)}, u32[]{:S(2)}, u32[]{:S(2)}) async-start(bf16[64,18,1024]{2,1,0:T(8,128)(2,1)} %stack.19), calls=%async_computation | async-start | bytes 6291456 | tf_op jit(solution)/shard_map/all_to_all | solution.py:13
  42.9 2.5 pad_slice_fusion
  45.4 2.0 reshape.197
  48.3 2.0 reshape.198
  51.7 2.0 reshape.199
  61.9 2.0 reshape.202
  79.4 2.5 copy.251
  81.8 2.5 reshape.206
  85.4 17.5 %psum.28 = f32[2,288]{1,0:T(2,128)S(1)} all-reduce(f32[2,288]{1,0:T(2,128)S(1)} %fusion.54), channel_id=1, replica_groups=mesh['ctx'=64,'tp'=8] {'tp'}, use_global_device_ids=true, to_apply=%region_1.2 | all-reduce | flops 576 | bytes 4608 | tf_op jit(solution)/shard_map/psum | solution.py:105
  103.2 2.3 add_convert_fusion
  106.5 2.1 collective-permute-start
  114.3 13.0 %collective-permute-done = bf16[14,14,144]{2,1,0:T(8,128)(2,1)} collective-permute-done((bf16[14,14,144]{2,1,0:T(8,128)(2,1)}, bf16[14,14,144]{2,1,0:T(8,128)(2,1)}, u32[]{:S(2)}, u32[]{:S(2)}) %collective-permute-start) | collective-permute-done | bytes 56480 | tf_op jit(solution)/shard_map/ppermute | solution.py:20
  132.1 2.3 reshape.210
  134.4 3.2 %fusion.29 = f32[64,1152]{1,0:T(8,128)} fusion(bf16[1152,1024]{1,0:T(8,128)(2,1)} %reshape.210, bf16[64,1,1024]{2,1,0:T(2,128)(2,1)S(1)} %reshape.237, bf16[64]{0:T(256)(128)(2,1)} %compare_convert_fusion), kind=kOutput, calls=%fused_computation.70 | convolution fusion | flops 151060480 | bytes 2785408 | tf_op jit(solution)/shard_map/dot_general | solution.py:81
  137.6 5.5 %copy.255 = bf16[1152,8,144]{0,2,1:T(8,128)(2,1)S(1)} copy(bf16[1152,8,144]{2,1,0:T(8,128)(2,1)} %all-gather.2.cloned.1.call-done) | data formatting | bytes 5308416 | tf_op jit(solution)/shard_map/all_gather | solution.py:110
  144.7 78.2 %all-reduce.14.cloned.1.call-done = (f32[64,1152]{1,0:T(8,128)}, f32[64,1152]{1,0:T(8,128)}) async-done(((f32[64,1152]{1,0:T(8,128)}, f32[64,1152]{1,0:T(8,128)}), (f32[64,1152]{1,0:T(8,128)}, f32[64,1152]{1,0:T(8,128)})) %all-reduce.14.cloned.1.call-update) | async-done | bytes 589840 | tf_op jit(solution)/shard_map/psum | solution.py:151
  222.9 2.3 convolution_bitcast_fusion.14
  226.4 2.1 collective-permute-start.1
  230.7 11.2 %all-to-all-start.1 = ((bf16[64,2,512]{2,1,0:T(2,128)(2,1)}), bf16[64,2,512]{2,1,0:T(2,128)(2,1)S(1)}, u32[]{:S(2)}, u32[]{:S(2)}) async-start(bf16[64,2,512]{2,1,0:T(2,128)(2,1)} %reshape.238), calls=%async_computation.1 | async-start | bytes 262144 | tf_op jit(solution)/shard_map/all_to_all | solution.py:146
  242.7 16.8 %psum.31 = f32[2,288]{1,0:T(2,128)S(1)} all-reduce(f32[2,288]{1,0:T(2,128)S(1)} %fusion.39), channel_id=1, replica_groups=mesh['ctx'=64,'tp'=8] {'tp'}, use_global_device_ids=true, to_apply=%region_8.9 | all-reduce | flops 576 | bytes 4608 | tf_op jit(solution)/shard_map/psum | solution.py:162
  289.9 2.5 fusion.15
  (192 shorter events, 82.5 us)
Async XLA Ops:
  7.2 95.8 %copy-start = (bf16[288,144]{0,1:T(8,128)(2,1)S(1)}, bf16[288,144]{0,1:T(8,128)(2,1)}, u32[]{:S(2)}) copy-start(bf16[288,144]{0,1:T(8,128)(2,1)} %param.12) | copy-start | bytes 248836
  7.2 130.5 %all-gather.2.cloned.1.call-start = ((), (), s32[]{:S(2)}) async-start(), calls=%async_computation.3 | async-start | bytes 4792320 | tf_op jit(solution)/shard_map/all_gather | solution.py:110
  10.7 22.9 %all-to-all-start.2 = ((bf16[64,2,512]{2,1,0:T(2,128)(2,1)}), bf16[64,2,512]{2,1,0:T(2,128)(2,1)S(1)}, u32[]{:S(2)}, u32[]{:S(2)}) async-start(bf16[64,2,512]{2,1,0:T(2,128)(2,1)} %reshape.236), calls=%async_computation.2 | async-start | bytes 262144 | tf_op jit(solution)/shard_map/all_to_all | solution.py:148
  36.5 95.6 %all-to-all-start = ((bf16[64,18,1024]{2,1,0:T(8,128)(2,1)}), bf16[64,18,1024]{2,1,0:T(8,128)(2,1)S(1)}, u32[]{:S(2)}, u32[]{:S(2)}) async-start(bf16[64,18,1024]{2,1,0:T(8,128)(2,1)} %stack.19), calls=%async_computation | async-start | bytes 6291456 | tf_op jit(solution)/shard_map/all_to_all | solution.py:13
  42.9 180.0 %all-reduce.14.cloned.1.call-start = ((), (), s32[]{:S(2)}) async-start(), calls=%async_computation.4 | async-start | bytes 1179648 | tf_op jit(solution)/shard_map/psum | solution.py:151
  48.3 26.5 %copy-start.16 = (bf16[1,144,48]{2,1,0:T(8,128)(2,1)}, bf16[1,144,48]{2,1,0:T(8,128)(2,1)S(1)}, u32[]{:S(2)}) copy-start(bf16[1,144,48]{2,1,0:T(8,128)(2,1)S(1)} %copy.234) | copy-start | bytes 41476
  79.3 29.2 %copy-start.39 = (s32[128]{0:T(128)S(1)}, s32[128]{0:T(128)}, u32[]{:S(2)}) copy-start(s32[128]{0:T(128)} %param.15) | copy-start | bytes 1540
  79.4 33.0 %copy-start.40 = (s32[16]{0:T(128)S(1)}, s32[16]{0:T(128)}, u32[]{:S(2)}) copy-start(s32[16]{0:T(128)} %param.16) | copy-start | bytes 196
  102.9 26.7 %copy-start.35 = (f32[2,288]{1,0:T(2,128)}, f32[2,288]{1,0:T(2,128)S(1)}, u32[]{:S(2)}) copy-start(f32[2,288]{1,0:T(2,128)S(1)} %psum.28) | copy-start | bytes 6916
  103.2 26.4 %copy-start.33 = (f32[2,144]{1,0:T(2,128)}, f32[2,144]{1,0:T(2,128)S(1)}, u32[]{:S(2)}) copy-start(f32[2,144]{1,0:T(2,128)S(1)} %fusion.10) | copy-start | bytes 3460
  106.5 20.8 %collective-permute-start = (bf16[14,14,144]{2,1,0:T(8,128)(2,1)}, bf16[14,14,144]{2,1,0:T(8,128)(2,1)}, u32[]{:S(2)}, u32[]{:S(2)}) collective-permute-start(bf16[14,14,144]{2,1,0:T(8,128)(2,1)} %bitcast.208), channel_id=1, source_target_pairs={{0,8},{8,16},{16,24},{24,32},{32,40},{40,48},{48,56},{56,64},{64,7... | collective-permute-start | bytes 169352 | tf_op jit(solution)/shard_map/ppermute | solution.py:20
  137.6 5.6 %copy-start.13 = (bf16[64,1152]{1,0:T(8,128)(2,1)S(1)}, bf16[64,1152]{1,0:T(8,128)(2,1)}, u32[]{:S(2)}) copy-start(bf16[64,1152]{1,0:T(8,128)(2,1)} %reshape.208) | copy-start | bytes 442372
  222.9 5.6 %copy-start.1 = (bf16[1152,1024]{1,0:T(8,128)(2,1)S(1)}, bf16[1152,1024]{1,0:T(8,128)(2,1)}, u32[]{:S(2)}) copy-start(bf16[1152,1024]{1,0:T(8,128)(2,1)} %reshape.210) | copy-start | bytes 7077892
  222.9 5.6 %copy-start.37 = (bf16[64]{0:T(256)(128)(2,1)S(1)}, bf16[64]{0:T(256)(128)(2,1)}, u32[]{:S(2)}) copy-start(bf16[64]{0:T(256)(128)(2,1)} %compare_convert_fusion) | copy-start | bytes 388
  222.9 5.6 %copy-start.38 = (f32[64,1152]{1,0:T(8,128)S(1)}, f32[64,1152]{1,0:T(8,128)}, u32[]{:S(2)}) copy-start(f32[64,1152]{1,0:T(8,128)} %get-tuple-element.15) | copy-start | bytes 884740
  226.4 15.7 %copy-start.3 = (f32[2,14,14,144]{3,0,2,1:T(2,128)S(1)}, f32[2,14,14,144]{3,0,2,1:T(2,128)}, u32[]{:S(2)}) copy-start(f32[2,14,14,144]{3,0,2,1:T(2,128)} %get-tuple-element.17) | copy-start | bytes 677380
  226.4 33.1 %copy-start.32 = (bf16[144,288]{1,0:T(8,128)(2,1)S(1)}, bf16[144,288]{1,0:T(8,128)(2,1)}, u32[]{:S(2)}) copy-start(bf16[144,288]{1,0:T(8,128)(2,1)} %param.11) | copy-start | bytes 248836
  226.4 33.1 %copy-start.36 = (f32[2,288]{1,0:T(2,128)S(1)}, f32[2,288]{1,0:T(2,128)}, u32[]{:S(2)}) copy-start(f32[2,288]{1,0:T(2,128)} %copy-done.35) | copy-start | bytes 6916
  226.4 15.5 %collective-permute-start.1 = (bf16[14,14,144]{2,1,0:T(8,128)(2,1)S(1)}, bf16[14,14,144]{2,1,0:T(8,128)(2,1)S(1)}, u32[]{:S(2)}, u32[]{:S(2)}) collective-permute-start(bf16[14,14,144]{2,1,0:T(8,128)(2,1)S(1)} %fusion.31), channel_id=1, source_target_pairs={{8,0},{16,8},{24,16},{32,24},{40,32},{48,40},{56,48},{64,56},{72,6... | collective-permute-start | bytes 169352 | tf_op jit(solution)/shard_map/ppermute | solution.py:20
  229.1 31.1 %copy-start.2 = (f32[2,14,14,3,48]{4,2,1,0,3:T(8,128)S(1)}, f32[2,14,14,3,48]{4,2,1,0,3:T(8,128)}, u32[]{:S(2)}) copy-start(f32[2,14,14,3,48]{4,2,1,0,3:T(8,128)} %get-tuple-element.41) | copy-start | bytes 677380
  230.7 62.5 %all-to-all-start.1 = ((bf16[64,2,512]{2,1,0:T(2,128)(2,1)}), bf16[64,2,512]{2,1,0:T(2,128)(2,1)S(1)}, u32[]{:S(2)}, u32[]{:S(2)}) async-start(bf16[64,2,512]{2,1,0:T(2,128)(2,1)} %reshape.238), calls=%async_computation.1 | async-start | bytes 262144 | tf_op jit(solution)/shard_map/all_to_all | solution.py:146
  241.9 18.8 %copy-start.17 = (bf16[1,144,48]{2,1,0:T(8,128)(2,1)S(1)}, bf16[1,144,48]{2,1,0:T(8,128)(2,1)}, u32[]{:S(2)}) copy-start(bf16[1,144,48]{2,1,0:T(8,128)(2,1)} %copy-done.16) | copy-start | bytes 41476
  242.7 19.1 %copy-start.19 = (bf16[1,144,48]{2,1,0:T(8,128)(2,1)S(1)}, bf16[1,144,48]{2,1,0:T(8,128)(2,1)}, u32[]{:S(2)}) copy-start(bf16[1,144,48]{2,1,0:T(8,128)(2,1)} %copy.236) | copy-start | bytes 41476
  260.8 5.5 %copy-start.27 = (bf16[1,144,48]{2,1,0:T(8,128)(2,1)S(1)}, bf16[1,144,48]{2,1,0:T(8,128)(2,1)}, u32[]{:S(2)}) copy-start(bf16[1,144,48]{2,1,0:T(8,128)(2,1)} %copy.245) | copy-start | bytes 41476
  (24 other events, 57.4 us)
Sparse Core Ops, SparseCore 0:
  11.3 108.2 all-gather.1
  144.7 78.1 all-reduce.13
